TPU v7x, 768 devices: a whole 4x8x12 slice. The times are simulated.
768 devices in a mesh: rep: 12 (over x, z_lo), fsdp: 64 (over y, z_hi, core).
Axes of the slice: x: 4, y: 8, z: 12 (z_hi: 4, z_lo: 3; z = z_hi * 3 + z_lo), core: 2. Of those that a mesh axis runs over, the one named last changes fastest.
Arguments:
- activations: bfloat16 [98304, 8192], P(('rep', 'fsdp')), may hold values from -54 to 54, as said below
- out_grad: bfloat16 [98304, 128], P(('rep', 'fsdp')), may hold values from -12 to 12
- key_weight: bfloat16 [8192, 128], P('fsdp'), may hold values from -0.0625 to 0.0625
- lengths: int32 [768, 8], P(('rep', 'fsdp')), may hold values from 0 to 128, as said below
Outputs:
- grad_in: bfloat16 [98304, 8192], P(('rep', 'fsdp'))
- weight_grad: float32 [8192, 128], P('fsdp')
- factor: float32 [1024, 1024], P('fsdp')
Inputs may be any that keep to these rules, and one draw needn't show every extreme that they name: Row d lists, in order, the lengths of the sequences packed from the start of device d's 128 token slots, zero for unused entries; slots past a row's sum are padding. Each row sums to between 1 and 128; the last row holds one sequence of exactly 128 and zeros. `activations`: activations are finite and within the stated range.
All inputs are finite; a program needn't handle non-finite values.
Results may differ from a plain program's by a relative error of at most 0.0015.
Values may be sent and summed in bfloat16 or wider, within the bound.
A program may use at most 64 MiB of HBM per device.

v0:
```python
import jax
import jax.numpy as jnp
from jax import lax
from jax.sharding import PartitionSpec as P

FBLK = 1024


def shards(activations, out_grad, key_weight, lengths):
    tok_rows = activations.shape[0]
    counts = lengths[0]
    ends = jnp.cumsum(counts)
    starts = ends - counts
    position = jnp.arange(tok_rows, dtype=jnp.int32)[:, None]
    member = (position >= starts[None, :]) & (position < ends[None, :])
    inverse = 1.0 / jnp.maximum(counts, 1).astype(jnp.float32)
    ratio = jnp.sum(jnp.where(member, inverse[None, :], jnp.float32(0.0)), axis=1)
    local_valid = jnp.sum(counts).astype(jnp.float32)
    local_seqs = jnp.sum((counts > 0).astype(jnp.float32))
    total_valid, total_seqs = lax.psum((local_valid, local_seqs), ("rep", "fsdp"))
    scale = total_valid / total_seqs
    scaled_grad = (out_grad.astype(jnp.float32) * ratio[:, None]).astype(jnp.bfloat16)
    product = lax.dot_general(
        scaled_grad,
        lax.all_gather(key_weight, "fsdp", axis=0, tiled=True),
        (((1,), (1,)), ((), ())),
        preferred_element_type=jnp.float32,
    )
    grad_in = (scale * product).astype(jnp.bfloat16)
    block = activations[:, :FBLK]
    weighted_block = (block.astype(jnp.float32) * ratio[:, None]).astype(jnp.bfloat16)
    columns = activations
    grad_sum = lax.psum_scatter(
        lax.dot_general(
            columns, scaled_grad, (((0,), (0,)), ((), ())), preferred_element_type=jnp.float32
        ),
        "fsdp",
        scatter_dimension=0,
        tiled=True,
    )
    columns = block
    factor_sum = lax.psum_scatter(
        lax.dot_general(
            columns, weighted_block, (((0,), (0,)), ((), ())), preferred_element_type=jnp.float32
        ),
        "fsdp",
        scatter_dimension=0,
        tiled=True,
    )
    grad_total, factor_total = lax.psum((grad_sum, factor_sum), "rep")
    return (grad_in, scale * grad_total, factor_total / total_seqs)


def solution(mesh):
    in_specs = (
        P(("rep", "fsdp"), None),
        P(("rep", "fsdp"), None),
        P("fsdp", None),
        P(("rep", "fsdp"), None),
    )
    out_specs = (P(("rep", "fsdp"), None), P("fsdp", None), P("fsdp", None))
    return jax.shard_map(shards, mesh=mesh, in_specs=in_specs, out_specs=out_specs, check_vma=False)
```

profile of v0, /device:TPU:1, one launch (start us, length us, event | category | flops | bytes accessed | tf_op | source)
XLA Modules:
  0.0 605.0 jit_solution(8041345633016550276)
XLA Ops:
  7.2 0.0 reduce-scatter.7.cloned.1.call-start
  7.2 1.3 divide_bitcast_fusion
  8.5 0.8 reduce-window.4
  9.3 1.3 fusion.5
  10.6 0.1 select_reduce_fusion
  10.7 3.8 convolution_bitcast_fusion.1
  14.5 5.3 copy.13
  19.9 0.0 copy-start
  19.9 0.0 copy-start.1
  19.9 0.0 reduce-scatter.7.cloned.1.call-update
  19.9 0.0 reduce-scatter.5.cloned.1.call-start
  19.9 1.5 copy-done
  21.5 0.0 copy-done.1
  21.5 2.7 convolution_bitcast_fusion
  24.2 0.0 reduce-scatter.5.cloned.1.call-update
  24.2 0.0 all-gather.2.cloned.1.call-start
  24.3 0.7 all-gather.2.cloned.1.call-update
  24.9 0.0 all-reduce.4.cloned.1.call-start
  25.6 121.7 %all-reduce = (f32[]{:T(128)}, f32[]{:T(128)}) all-reduce(f32[]{:T(128)S(6)} %convert_element_type.26, f32[]{:T(128)} %get-tuple-element.19), channel_id=1, replica_groups=mesh['rep'=12,'fsdp'=64] {'rep','fsdp'}, use_global_device_ids=true, to_apply=%region_1.2 | all-reduce | flops 2 | bytes 16 | tf_op jit(solution)/shard_map/psum | solution.py:20
  148.7 46.4 %reduce-scatter.7.cloned.1.call-done = f32[16,1024]{1,0:T(8,128)} async-done(((f32[1024,1024]{1,0:T(8,128)}), f32[16,1024]{1,0:T(8,128)}) %reduce-scatter.7.cloned.1.call-update) | async-done | bytes 65552
  195.1 1.8 copy.14
  197.0 172.6 %reduce-scatter.5.cloned.1.call-done = f32[128,128]{0,1:T(8,128)} async-done(((f32[8192,128]{0,1:T(8,128)}), f32[128,128]{0,1:T(8,128)}) %reduce-scatter.5.cloned.1.call-update) | async-done | bytes 65552 | tf_op jit(solution)/shard_map/reduce_scatter | solution.py:33
  369.6 0.0 all-reduce.4.cloned.1.call-update
  369.6 98.2 %all-gather.2.cloned.1.call-done = bf16[8192,128]{1,0:T(8,128)(2,1)} async-done(((bf16[128,128]{1,0:T(8,128)(2,1)}), bf16[8192,128]{1,0:T(8,128)(2,1)}) %all-gather.2.cloned.1.call-update) | async-done | bytes 2097168 | tf_op jit(solution)/shard_map/all_gather | solution.py:25
  467.8 3.7 fusion
  471.5 122.8 %all-reduce.4.cloned.1.call-done = (f32[128,128]{0,1:T(8,128)}, f32[16,1024]{0,1:T(8,128)}) async-done(((f32[128,128]{0,1:T(8,128)}, f32[16,1024]{0,1:T(8,128)}), (f32[128,128]{0,1:T(8,128)}, f32[16,1024]{0,1:T(8,128)})) %all-reduce.4.cloned.1.call-update) | async-done | bytes 131088 | tf_op jit(solution)/shard_map/psum | solution.py:50
  594.3 0.8 broadcast_multiply_fusion
  595.1 0.7 copy.11
  595.8 1.8 broadcast_divide_fusion
  597.6 0.8 copy.12
Async XLA Ops:
  7.2 188.0 %reduce-scatter.7.cloned.1.call-start = ((), (), s32[]{:S(2)}) async-start(), calls=%async_computation.4 | async-start | bytes 4259840
  19.9 1.6 copy-start
  19.9 1.6 copy-start.1
  19.9 349.7 %reduce-scatter.5.cloned.1.call-start = ((), (), s32[]{:S(2)}) async-start(), calls=%async_computation.3 | async-start | bytes 4259840 | tf_op jit(solution)/shard_map/reduce_scatter | solution.py:33
  24.2 443.6 %all-gather.2.cloned.1.call-start = ((), (), s32[]{:S(2)}) async-start(), calls=%async_computation.2 | async-start | bytes 2129920 | tf_op jit(solution)/shard_map/all_gather | solution.py:25
  24.9 569.3 %all-reduce.4.cloned.1.call-start = ((), (), s32[]{:S(2)}) async-start(), calls=%async_computation.5 | async-start | bytes 1179648 | tf_op jit(solution)/shard_map/psum | solution.py:50
Sparse Core Ops, SparseCore 0:
  20.0 175.0 reduce-scatter.6
  201.3 168.2 reduce-scatter.4
  373.5 94.3 all-gather.1
  471.0 123.2 all-reduce.3
where the time goes:
time: 616 us; the launch traced here: 605 us
  waiting for transfers between devices  441 us (72%)
  blocking collectives  122 us (20%)
  between operations  15.8 us (3%)
  matrix products  10.2 us (2%)
  local copies, waits for them, and re-layouts  10.2 us (2%)
    reduce_scatter x1, waiting for transfers between devices, shards(): lax.psum_scatter(lax.dot_general(columns, scaled_grad, (((0,), (0,)), (()...  173 us
    psum x1, waiting for transfers between devices, shards(): grad_total, factor_total = lax.psum((grad_sum, factor_sum), 'rep')  123 us
    psum x1, blocking collectives, shards(): lax.psum((local_valid, local_seqs), ('rep', 'fsdp'))  122 us
    all_gather x1, waiting for transfers between devices, shards(): lax.all_gather(key_weight, 'fsdp', axis=0, tiled=True)  98.2 us
    unnamed x5, waiting for transfers between devices  47.1 us
  transfers between devices with their start and end apart: 4, of which 4 were waited for; matrix products, arithmetic and copies ran while one was open for 1% of the time, Pallas kernels for 0%

commit v1 on v0

v1 whole, which is shorter than its diff:
```python
import jax
import jax.numpy as jnp
from jax import lax
from jax.experimental import pallas as pl
from jax.experimental.pallas import tpu as pltpu
from jax.sharding import PartitionSpec as P

FBLK = 1024
X, Y, ZH, ZL = 4, 8, 4, 3
Z = ZH * ZL
T = 128
MESH = pl.DeviceIdType.MESH
F32, BF16 = jnp.float32, jnp.bfloat16


def ratio_of(tile):
    pos = lax.broadcasted_iota(jnp.int32, (T, T), 0)
    end = jnp.zeros((1, T), jnp.int32)
    ratio = jnp.zeros((T, T), F32)
    for s in range(8):
        length = tile[s:s + 1, :]
        start, end = end, end + length
        inverse = 1.0 / jnp.maximum(length, 1).astype(F32)
        ratio = ratio + jnp.where((pos >= start) & (pos < end), inverse, 0.0)
    return ratio


def kernel(
    act, og, kw, lens, grad_in, wgrad, factor,
    abuf, sgt, sgs, psum, xr, ybuf, yr, yl, gblk, wbt, lt, cy, cz,
    wbuf, gbuf, zbuf, zr, lr, finw, finf, fw, ff, ogv, ss, rs, ls,
):
    rep, fs = lax.axis_index("rep"), lax.axis_index("fsdp")
    x, zl = lax.div(rep, ZL), lax.rem(rep, ZL)
    y, zh, c = lax.div(fs, 8), lax.rem(lax.div(fs, 2), ZH), lax.rem(fs, 2)
    z = zh * ZL + zl

    def dev(dx=0, dy=0, dz=0, dc=0, dzh=0, dzl=0):
        x2, y2 = lax.rem(x + dx, X), lax.rem(y + dy, Y)
        if dz:
            z2 = lax.rem(z + dz, Z)
            zh2, zl2 = lax.div(z2, ZL), lax.rem(z2, ZL)
        else:
            zh2, zl2 = lax.rem(zh + dzh, ZH), lax.rem(zl + dzl, ZL)
        c2 = 1 - c if dc else c
        return (x2 * ZL + zl2, y2 * 8 + zh2 * 2 + c2)

    sib, right, left = dev(dc=1), dev(dx=1), dev(dx=3)
    up, down = dev(dy=1), dev(dy=7)
    group = [right, left, dev(dx=2), sib, dev(dx=1, dc=1), dev(dx=3, dc=1), dev(dx=2, dc=1)]
    count = [0]
    sent = []

    def send(src, dst, to):
        k = count[0]
        count[0] += 1
        copy = pltpu.make_async_remote_copy(
            src_ref=src, dst_ref=dst, send_sem=ss.at[k], recv_sem=rs.at[k],
            device_id=to, device_id_type=MESH,
        )
        copy.start()
        sent.append(copy)
        return copy

    def cols(b):
        return act.at[:, pl.ds(pl.multiple_of(b * T, T), T)]

    def start_own(i, _):
        pltpu.make_async_copy(cols(2 * i + c), abuf.at[i, 0], ls.at[0]).start()
        return 0

    lax.fori_loop(0, 32, start_own, 0)
    own_all = pltpu.make_async_copy(abuf.at[:, 0], abuf.at[:, 0], ls.at[0])
    og_copy = pltpu.make_async_copy(og, ogv, ls.at[1])
    og_copy.start()
    w_copy = pltpu.make_async_copy(kw, wbuf.at[y, zh, c], ls.at[2])
    w_copy.start()
    blk_copy = pltpu.make_async_copy(act.at[:, 0:FBLK], gblk.at[0], ls.at[3])
    blk_copy.start()

    barrier = pltpu.get_barrier_semaphore()
    peers = group + [dev(dy=d) for d in range(1, Y)] + [dev(dz=d) for d in range(1, Z)]
    for peer in peers:
        pl.semaphore_signal(barrier, inc=1, device_id=peer, device_id_type=MESH)
    pl.semaphore_wait(barrier, len(peers))

    g_r = send(act.at[:, 0:FBLK], gblk.at[1], right)
    g_l = send(act.at[:, 0:FBLK], gblk.at[2], left)
    act_k = count[0]
    count[0] += 2

    def swap(half):
        k = act_k + half

        def start(i, _):
            pltpu.make_async_remote_copy(
                src_ref=cols(2 * i + 1 - c), dst_ref=abuf.at[i, 1], send_sem=ss.at[k], recv_sem=rs.at[k],
                device_id=sib, device_id_type=MESH,
            ).start()
            return 0

        lax.fori_loop(16 * half, 16 * half + 16, start, 0)
        part = abuf.at[16 * half:16 * half + 16]
        whole = pltpu.make_async_remote_copy(
            src_ref=part.at[:, 0], dst_ref=part.at[:, 1], send_sem=ss.at[k], recv_sem=rs.at[k],
            device_id=sib, device_id_type=MESH,
        )
        sent.append(whole)
        return whole

    swap_a, swap_b = swap(0), swap(1)
    w_zh = [send(kw, wbuf.at[y, zh, c], dev(dzh=d)) for d in range(1, ZH)]

    row = lax.broadcasted_iota(jnp.int32, (8, T), 0)
    tile = jnp.zeros((8, T), jnp.int32)
    for s in range(8):
        tile = jnp.where(row == s, lens[0, s], tile)
    lt[0] = tile
    l_copies = [send(lt.at[0], lt.at[1 + i], to) for i, to in enumerate(group)]
    og_copy.wait()
    scaled = ogv[...].astype(F32) * ratio_of(tile)
    sgs[...] = scaled.astype(BF16)
    sgt[0] = scaled.T.astype(BF16)
    s_copy = send(sgt.at[0], sgt.at[1], sib)
    blk_copy.wait()
    g_s = [send(gblk.at[0], gblk.at[4], sib)]

    own_all.wait()
    s_copy.wait_recv()
    heads = jnp.concatenate([sgt[0], sgt[1]], axis=1)

    def weight_block(i, _):
        out = jnp.dot(heads, abuf[i].reshape(2 * T, T), preferred_element_type=F32)
        psum[:, i] = out.reshape(X, 32, T)
        return 0

    xp, xm, xo = lax.rem(x + 1, X), lax.rem(x + 3, X), lax.rem(x + 2, X)
    swap_a.wait_recv()
    lax.fori_loop(0, 16, weight_block, 0)
    r1 = send(psum.at[xo, 0:16], xr.at[0], right)
    l2 = None
    swap_b.wait_recv()
    lax.fori_loop(16, 32, weight_block, 0)
    l1 = send(psum.at[xo, 16:32], xr.at[1], left)
    r2 = send(psum.at[xp, 16:32], xr.at[2], right)
    l2 = send(psum.at[xm, 0:16], xr.at[3], left)

    w_copy.wait()
    for copy in w_zh:
        copy.wait_recv()

    def w_step(s):
        lo, hi = lax.rem(y + Y - s, Y), lax.rem(y + s, Y)
        if s < 3:
            return [
                send(wbuf.at[lo, :, c], wbuf.at[lo, :, c], up),
                send(wbuf.at[hi, :, c], wbuf.at[hi, :, c], down),
            ]
        return [
            send(wbuf.at[lo, 0:2, c], wbuf.at[lo, 0:2, c], up),
            send(wbuf.at[hi, 2:4, c], wbuf.at[hi, 2:4, c], down),
        ]

    def arrived(copies):
        for copy in copies:
            copy.wait_recv()

    w_now = w_step(0)

    arrived(l_copies)
    every = lt[...]
    cy[0, 0:8] = jnp.sum(every, axis=0).astype(F32)
    cy[0, 8:16] = jnp.sum((every > 0).astype(jnp.int32), axis=0).astype(F32)
    y_counts = [send(cy.at[0], cy.at[d], dev(dy=d)) for d in range(1, Y)]

    g_r.wait_recv()
    f_r = send(gblk.at[1, 0:64], gblk.at[3, 0:64], right)
    g_l.wait_recv()
    f_l = send(gblk.at[2, 64:128], gblk.at[3, 64:128], left)
    g_s.append(send(gblk.at[1], gblk.at[5], sib))
    g_s.append(send(gblk.at[2], gblk.at[6], sib))

    arrived(y_counts)
    cz[0] = jnp.sum(cy[...], axis=0)
    z_counts = [send(cz.at[0], cz.at[d], dev(dz=d)) for d in range(1, Z)]

    arrived(w_now)
    w_now = w_step(1)

    r1.wait_recv()
    psum[xp, 0:16] += xr[0]
    r3 = send(psum.at[xp, 0:16], xr.at[4], right)
    l1.wait_recv()
    psum[xm, 16:32] += xr[1]
    l3 = send(psum.at[xm, 16:32], xr.at[5], left)

    arrived(w_now)
    w_now = w_step(2)

    arrived([f_r, f_l])
    g_s.append(send(gblk.at[3], gblk.at[7], sib))
    mine = pl.ds(pl.multiple_of((2 * x + c) * T, T), T)

    def weigh(s):
        weighted = gblk[s, :, mine].astype(F32) * ratio_of(lt[s])
        wbt[:, s * T:(s + 1) * T] = weighted.T.astype(BF16)

    for s in range(4):
        weigh(s)
    for s in range(4):
        g_s[s].wait_recv()
        weigh(4 + s)

    def factor_block(i, _):
        part = gblk[:, :, pl.ds(pl.multiple_of(i * T, T), T)].reshape(8 * T, T)
        ybuf[1, i] = jnp.dot(wbt[...], part, preferred_element_type=F32)
        return 0

    lax.fori_loop(0, Y, factor_block, 0)

    def y_step(p, s, before):
        t = 4 - s
        hi, lo = lax.rem(y + t, Y), lax.rem(y + Y - t, Y)
        if s == 0:
            return [
                send(ybuf.at[p, hi, 0:64], yr.at[p, 0, 0:64], up),
                send(ybuf.at[p, hi, 64:128], yl.at[p, 0, 64:128], down),
            ]
        before[0].wait_recv()
        if s == 1:
            ybuf[p, hi, 0:64] += yr[p, 0, 0:64]
        else:
            ybuf[p, hi] += yr[p, s - 1]
        a = send(ybuf.at[p, hi], yr.at[p, s], up)
        before[1].wait_recv()
        if s == 1:
            ybuf[p, lo, 64:128] += yl[p, 0, 64:128]
        else:
            ybuf[p, lo] += yl[p, s - 1]
        b = send(ybuf.at[p, lo], yl.at[p, s], down)
        return [a, b]

    f_y = y_step(1, 0, None)
    arrived(w_now)
    w_now = w_step(3)
    f_y = y_step(1, 1, f_y)

    l2.wait_recv()
    r3.wait_recv()
    ybuf[0, 0:4] = (psum[x, 0:16] + xr[3] + xr[4]).reshape(4, T, T)
    r2.wait_recv()
    l3.wait_recv()
    ybuf[0, 4:8] = (psum[x, 16:32] + xr[2] + xr[5]).reshape(4, T, T)
    g_y = y_step(0, 0, None)
    f_y = y_step(1, 2, f_y)
    arrived(w_now)
    w_swap = send(wbuf.at[:, :, c], wbuf.at[:, :, c], sib)
    g_y = y_step(0, 1, g_y)
    f_y = y_step(1, 3, f_y)

    arrived(z_counts)
    total = jnp.sum(cz[...], axis=0)
    valid = jnp.sum(total[0:8], axis=0, keepdims=True)
    seqs = jnp.sum(total[8:16], axis=0, keepdims=True)
    scale_row = valid / seqs
    scale = jnp.max(scale_row)

    g_y = y_step(0, 2, g_y)
    w_swap.wait_recv()

    def product(i):
        out = lax.dot_general(
            sgs[...], wbuf[i].reshape(1024, T), (((1,), (1,)), ((), ())), preferred_element_type=F32
        )
        gbuf[:, i * 1024:(i + 1) * 1024] = (scale * out).astype(BF16)

    for i in range(4):
        product(i)
    arrived(f_y)
    turned = (ybuf[1, y] + yr[1, 3] + yl[1, 3]).T
    zbuf[:, 32:64] = turned.reshape(ZH, 32, T)
    g_y = y_step(0, 3, g_y)
    for i in range(4, 8):
        product(i)
    out_copy = pltpu.make_async_copy(gbuf, grad_in, ls.at[4])
    out_copy.start()
    arrived(g_y)
    zbuf[:, 0:32] = (ybuf[0, y] + yr[0, 3] + yl[0, 3]).reshape(ZH, 32, T)

    z_copies = [send(zbuf.at[lax.rem(zh + d, ZH)], zr.at[d], dev(dzh=d)) for d in range(1, ZH)]
    zr[0] = zbuf[zh]
    arrived(z_copies)
    lr[0] = zr[0] + zr[1] + zr[2] + zr[3]
    l_sums = [send(lr.at[0], lr.at[d], dev(dzl=d)) for d in range(1, ZL)]
    arrived(l_sums)
    done = lr[0] + lr[1] + lr[2]
    finw[...] = done[0:32]
    finf[...] = done[32:64].reshape(2, 16, T)
    slot = 2 * x + c
    last = [send(finw, fw.at[x], to) for to in group[:3]]
    last += [send(finf.at[c], ff.at[slot], to) for to in group[:3]]
    last += [send(finf.at[1 - c], ff.at[slot], to) for to in group[3:]]
    fw[x] = done[0:32]
    ff[slot] = finf[c]
    arrived(last)
    wgrad[...] = scale * fw[...].reshape(T, T).T
    for g in range(8):
        factor[:, g * T:(g + 1) * T] = ff[g] / seqs
    out_copy.wait()
    for copy in sent:
        copy.wait_send()


def shards(activations, out_grad, key_weight, lengths):
    sems = 160
    any_space = pl.BlockSpec(memory_space=pl.ANY)
    vmem = pl.BlockSpec(memory_space=pltpu.VMEM)
    return pl.pallas_call(
        kernel,
        out_shape=(
            jax.ShapeDtypeStruct((T, 8192), BF16),
            jax.ShapeDtypeStruct((T, T), F32),
            jax.ShapeDtypeStruct((16, FBLK), F32),
        ),
        in_specs=[any_space, any_space, any_space, pl.BlockSpec(memory_space=pltpu.SMEM)],
        out_specs=(any_space, vmem, vmem),
        scratch_shapes=[
            pltpu.VMEM((32, 2, T, T), BF16),
            pltpu.VMEM((2, T, T), BF16),
            pltpu.VMEM((T, T), BF16),
            pltpu.VMEM((X, 32, 32, T), F32),
            pltpu.VMEM((6, 16, 32, T), F32),
            pltpu.VMEM((2, Y, T, T), F32),
            pltpu.VMEM((2, 4, T, T), F32),
            pltpu.VMEM((2, 4, T, T), F32),
            pltpu.VMEM((8, T, FBLK), BF16),
            pltpu.VMEM((T, 8 * T), BF16),
            pltpu.VMEM((8, 8, T), jnp.int32),
            pltpu.VMEM((Y, 16, T), F32),
            pltpu.VMEM((Z, 16, T), F32),
            pltpu.VMEM((Y, ZH, 2, T, T), BF16),
            pltpu.VMEM((T, 8192), BF16),
            pltpu.VMEM((ZH, 64, T), F32),
            pltpu.VMEM((ZH, 64, T), F32),
            pltpu.VMEM((ZL, 64, T), F32),
            pltpu.VMEM((32, T), F32),
            pltpu.VMEM((2, 16, T), F32),
            pltpu.VMEM((X, 32, T), F32),
            pltpu.VMEM((8, 16, T), F32),
            pltpu.VMEM((T, T), BF16),
            pltpu.SemaphoreType.DMA((sems,)),
            pltpu.SemaphoreType.DMA((sems,)),
            pltpu.SemaphoreType.DMA((8,)),
        ],
        compiler_params=pltpu.CompilerParams(
            collective_id=0, has_side_effects=True, vmem_limit_bytes=48 * 1024 * 1024
        ),
    )(activations, out_grad, key_weight, lengths)


def solution(mesh):
    in_specs = (
        P(("rep", "fsdp"), None),
        P(("rep", "fsdp"), None),
        P("fsdp", None),
        P(("rep", "fsdp"), None),
    )
    out_specs = (P(("rep", "fsdp"), None), P("fsdp", None), P("fsdp", None))
    return jax.shard_map(shards, mesh=mesh, in_specs=in_specs, out_specs=out_specs, check_vma=False)
```

time: 616 us -> 92.4 us (0.15); the launches traced: 605 us -> 92.1 us
  waiting for transfers between devices: 441 us -> 0 us
  blocking collectives: 122 us -> 0 us
  Pallas kernels: 0 us -> 85.1 us
  between operations: 15.8 us -> 0.65 us
  matrix products: 10.2 us -> 0 us
    reduce_scatter x1 -> x0, waiting for transfers between devices: 173 us -> none  [shards(): lax.psum_scatter(lax.dot_general(columns, scaled_grad, (((0,), (0,)), (()...]
    psum x1 -> x0, waiting for transfers between devices: 123 us -> none  [shards(): grad_total, factor_total = lax.psum((grad_sum, factor_sum), 'rep')]
    psum x1 -> x0, blocking collectives: 122 us -> none  [shards(): lax.psum((local_valid, local_seqs), ('rep', 'fsdp'))]
    all_gather x1 -> x0, waiting for transfers between devices: 98.2 us -> none  [shards(): lax.all_gather(key_weight, 'fsdp', axis=0, tiled=True)]
    pallas_call x0 -> x1, Pallas kernels: none -> 85.1 us  [shards(): pl.pallas_call(kernel, out_shape=(jax.ShapeDtypeStruct((T, 8192), BF16),...]
    unnamed x5 -> x0, waiting for transfers between devices: 47.1 us -> none
    dot_general x3 -> x0, matrix products: 10.2 us -> none  [the longest x1 3.83 us: shards(): lax.dot_general(columns, weighted_block, (((0,), (0,)), ((), ())), prefer...]
  transfers between devices with their start and end apart: 4 -> 0, of which waited for: 4 -> 0; matrix products, arithmetic and copies ran while one was open for 1% -> 0% of each run, Pallas kernels for 0% -> 0%
where the time goes in v1:
time: 92.4 us; the launch traced here: 92.1 us
  Pallas kernels  85.1 us (92%)
  local copies, waits for them, and re-layouts  6.33 us (7%)
    pallas_call x1, Pallas kernels, shards(): pl.pallas_call(kernel, out_shape=(jax.ShapeDtypeStruct((T, 8192), BF16),...  85.1 us
    unnamed x11, local copies, waits for them, and re-layouts  6.33 us

profile of v1, /device:TPU:1, one launch (start us, length us, event | category | flops | bytes accessed | tf_op | source)
XLA Modules:
  0.0 92.1 jit_solution(13053743394995554961)
XLA Ops:
  0.6 0.0 copy-start
  0.6 1.6 %copy-done = bf16[128,8192]{1,0:T(8,128)(2,1)S(1)} copy-done((bf16[128,8192]{1,0:T(8,128)(2,1)S(1)}, bf16[128,8192]{1,0:T(8,128)(2,1)}, u32[]{:S(2)}) %copy-start) | copy-done | bytes 2097176
  2.2 0.0 copy-start.1
  2.2 0.8 copy-done.1
  3.0 0.0 copy-start.2
  3.0 0.8 copy-done.2
  3.7 0.0 copy-start.3
  3.7 0.7 copy-done.3
  4.4 85.1 %shard_map.67 = (bf16[128,8192]{1,0:T(8,128)(2,1)S(1)}, f32[128,128]{1,0:T(8,128)S(1)}, f32[16,1024]{1,0:T(8,128)S(1)}) custom-call(bf16[128,8192]{1,0:T(8,128)(2,1)S(1)} %copy-done, bf16[128,128]{1,0:T(8,128)(2,1)S(1)} %copy-done.1, bf16[128,128]{1,0:T(8,128)(2,1)S(1)} %copy-done.2, s32[1,8]{1,0:T(1,128)S(1)} %copy-done.3), custom_call_target="tpu_custom_call" | custom-call | tf_op jit(solution)/shard_map/pallas_call | solution.py:318
  89.5 1.3 %copy.10 = bf16[128,8192]{1,0:T(8,128)(2,1)} copy(bf16[128,8192]{1,0:T(8,128)(2,1)S(1)} %get-tuple-element.6) | data formatting | bytes 4194304
  90.8 0.6 copy.11
  91.5 0.6 copy.12
Async XLA Ops:
  0.6 1.6 %copy-start = (bf16[128,8192]{1,0:T(8,128)(2,1)S(1)}, bf16[128,8192]{1,0:T(8,128)(2,1)}, u32[]{:S(2)}) copy-start(bf16[128,8192]{1,0:T(8,128)(2,1)} %act.1) | copy-start | bytes 6291460
  2.2 0.8 copy-start.1
  3.0 0.8 copy-start.2
  3.7 0.7 copy-start.3

commit v2 on v1

v2 whole, which is shorter than its diff:
```python
import jax
import jax.numpy as jnp
from jax import lax
from jax.experimental import pallas as pl
from jax.experimental.pallas import tpu as pltpu
from jax.sharding import PartitionSpec as P

FBLK = 1024
X, Y, ZH, ZL = 4, 8, 4, 3
T = 128
MESH = pl.DeviceIdType.MESH
F32, BF16 = jnp.float32, jnp.bfloat16


def ratio_of(tile):
    pos = lax.broadcasted_iota(jnp.int32, (T, T), 0)
    end = jnp.zeros((1, T), jnp.int32)
    ratio = jnp.zeros((T, T), F32)
    for s in range(8):
        length = tile[s:s + 1, :]
        start, end = end, end + length
        inverse = 1.0 / jnp.maximum(length, 1).astype(F32)
        ratio = ratio + jnp.where((pos >= start) & (pos < end), inverse, 0.0)
    return ratio


def kernel(
    act, og, kw, lens, grad_in, wgrad, factor,
    abuf, sgt, sgs, psum, xr, yb, ybr, ybl, ya, yar, yal, yf, yfr, yfl, xb, xbr, gblk, wbt, lt, cy, cz, cl,
    wbuf, zw, zwr, zf, zfr, lr, finw, finf, fw, ff, ogv, lens_s, ss, rs, ls,
):
    rep, fs = lax.axis_index("rep"), lax.axis_index("fsdp")
    x, zl = lax.div(rep, ZL), lax.rem(rep, ZL)
    y, zh, c = lax.div(fs, 8), lax.rem(lax.div(fs, 2), ZH), lax.rem(fs, 2)

    def dev(dx=0, dy=0, dzh=0, dzl=0, dc=0):
        c2 = 1 - c if dc else c
        x2, y2, zh2, zl2 = lax.rem(x + dx, X), lax.rem(y + dy, Y), lax.rem(zh + dzh, ZH), lax.rem(zl + dzl, ZL)
        return (x2 * ZL + zl2, y2 * 8 + zh2 * 2 + c2)

    sib, right, left = dev(dc=1), dev(dx=1), dev(dx=3)
    up, down = dev(dy=1), dev(dy=7)
    fore, back = dev(dzh=1), dev(dzh=3)
    group = [right, left, sib, dev(dx=1, dc=1), dev(dx=3, dc=1), dev(dx=2), dev(dx=2, dc=1)]
    same, other = [group[0], group[1], group[5]], [group[2], group[3], group[4], group[6]]
    ys = [dev(dy=d) for d in range(1, Y)]
    zhs = [dev(dzh=d) for d in range(1, ZH)]
    zls = [dev(dzl=d) for d in range(1, ZL)]
    count = [0]
    sent = []

    def send(src, dst, to):
        k = count[0]
        count[0] += 1
        copy = pltpu.make_async_remote_copy(
            src_ref=src, dst_ref=dst, send_sem=ss.at[k], recv_sem=rs.at[k],
            device_id=to, device_id_type=MESH,
        )
        copy.start()
        sent.append(copy)
        return copy

    def arrived(copies):
        for copy in copies:
            copy.wait_recv()

    lens_copy = pltpu.make_async_copy(lens, lens_s, ls.at[4])
    lens_copy.start()
    og_copy = pltpu.make_async_copy(og, ogv, ls.at[1])
    og_copy.start()

    barrier = pltpu.get_barrier_semaphore()
    peers = group + ys + zhs + zls
    for peer in peers:
        pl.semaphore_signal(barrier, inc=1, device_id=peer, device_id_type=MESH)

    def cols(i, half, core):
        b = lax.div(i, 2) * 8 + half * 4 + lax.rem(i, 2) * 2 + core
        return act.at[:, pl.ds(pl.multiple_of(b * T, T), T)]

    for half in range(2):
        def start_own(i, _, half=half):
            pltpu.make_async_copy(cols(i, half, c), abuf.at[16 * half + i, 0], ls.at[0]).start()
            return 0

        lax.fori_loop(0, 16, start_own, 0)
    own_all = pltpu.make_async_copy(abuf.at[:, 0], abuf.at[:, 0], ls.at[0])
    blk_copy = pltpu.make_async_copy(act.at[:, 0:FBLK], gblk.at[0], ls.at[3])
    blk_copy.start()
    part = pl.ds(pl.multiple_of(32 * x, 32), 32)
    w_copy = pltpu.make_async_copy(kw.at[part], wbuf.at[y, zh, c, part], ls.at[2])
    w_copy.start()

    lens_copy.wait()
    row = lax.broadcasted_iota(jnp.int32, (8, T), 0)
    tile = jnp.zeros((8, T), jnp.int32)
    for s in range(8):
        tile = jnp.where(row == s, lens_s[0, s], tile)
    lt[0] = tile
    og_copy.wait()
    scaled = ogv[...].astype(F32) * ratio_of(tile)
    sgs[...] = scaled.astype(BF16)
    sgt[0] = scaled.T.astype(BF16)

    pl.semaphore_wait(barrier, len(peers))

    act_k = count[0]
    count[0] += 2

    def swap(half):
        k = act_k + half

        def start(i, _):
            pltpu.make_async_remote_copy(
                src_ref=cols(i, half, 1 - c), dst_ref=abuf.at[16 * half + i, 1], send_sem=ss.at[k], recv_sem=rs.at[k],
                device_id=sib, device_id_type=MESH,
            ).start()
            return 0

        lax.fori_loop(0, 16, start, 0)
        part = abuf.at[16 * half:16 * half + 16]
        whole = pltpu.make_async_remote_copy(
            src_ref=part.at[:, 0], dst_ref=part.at[:, 1], send_sem=ss.at[k], recv_sem=rs.at[k],
            device_id=sib, device_id_type=MESH,
        )
        sent.append(whole)
        return whole

    s_copy = send(sgt.at[0], sgt.at[1], sib)
    swap_a = swap(1)
    g_r = send(act.at[:, 0:FBLK], gblk.at[1], right)
    g_l = send(act.at[:, 0:FBLK], gblk.at[2], left)
    swap_b = swap(0)
    w_y = [send(kw.at[part], wbuf.at[y, zh, c, part], to) for to in ys]
    l_copies = [send(lt.at[0], lt.at[1 + i], to) for i, to in enumerate(group)]

    own_all.wait()
    s_copy.wait_recv()
    heads = jnp.concatenate([sgt[0], sgt[1]], axis=1)

    def block(i):
        return jnp.dot(heads, abuf[i].reshape(2 * T, T), preferred_element_type=F32)

    def block_b(i, _):
        yb[lax.div(i, 2), pl.ds(pl.multiple_of(lax.rem(i, 2) * T, T), T)] = block(i)
        return 0

    def block_a(i, _):
        psum[:, i] = block(16 + i).reshape(X, 32, T)
        return 0

    def y_step(buf, up_buf, down_buf, s, before):
        n = buf.shape[1] // 2
        t = 4 - s
        hi, lo = lax.rem(y + t, Y), lax.rem(y + Y - t, Y)
        if s == 0:
            return [
                send(buf.at[hi, 0:n], up_buf.at[0, 0:n], up),
                send(buf.at[hi, n:2 * n], down_buf.at[0, n:2 * n], down),
            ]
        before[0].wait_recv()
        if s == 1:
            buf[hi, 0:n] += up_buf[0, 0:n]
        else:
            buf[hi] += up_buf[s - 1]
        a = send(buf.at[hi], up_buf.at[s], up)
        before[1].wait_recv()
        if s == 1:
            buf[lo, n:2 * n] += down_buf[0, n:2 * n]
        else:
            buf[lo] += down_buf[s - 1]
        b = send(buf.at[lo], down_buf.at[s], down)
        return [a, b]

    def step_b(s, before):
        return y_step(yb, ybr, ybl, s, before)

    def step_a(s, before):
        return y_step(ya, yar, yal, s, before)

    def step_f(s, before):
        return y_step(yf, yfr, yfl, s, before)

    xp, xm, xo = lax.rem(x + 1, X), lax.rem(x + 3, X), lax.rem(x + 2, X)
    swap_a.wait_recv()
    lax.fori_loop(0, 16, block_a, 0)
    r1 = send(psum.at[xo, 0:8], xr.at[0], right)
    l1 = send(psum.at[xo, 8:16], xr.at[1], left)
    blk_copy.wait()
    g_s = [send(gblk.at[0], gblk.at[3], sib)]
    swap_b.wait_recv()
    lax.fori_loop(0, 16, block_b, 0)
    b_y = step_b(0, None)

    g_r.wait_recv()
    f_r = send(gblk.at[1, 0:64], gblk.at[6, 0:64], right)
    g_l.wait_recv()
    f_l = send(gblk.at[2, 64:128], gblk.at[6, 64:128], left)
    g_s.append(send(gblk.at[1], gblk.at[4], sib))
    g_s.append(send(gblk.at[2], gblk.at[5], sib))
    r2 = send(psum.at[xp, 8:16], xr.at[2], right)
    l2 = send(psum.at[xm, 0:8], xr.at[3], left)

    w_copy.wait()
    arrived(w_y)
    w_z = [
        send(wbuf.at[:, zh, c, part], wbuf.at[:, zh, c, part], fore),
        send(wbuf.at[:, zh, c, part], wbuf.at[:, zh, c, part], back),
    ]

    arrived(l_copies)
    every = lt[...]
    cy[0, 0:8] = jnp.sum(every, axis=0).astype(F32)
    cy[0, 8:16] = jnp.sum((every > 0).astype(jnp.int32), axis=0).astype(F32)
    y_counts = [send(cy.at[0], cy.at[1 + i], to) for i, to in enumerate(ys)]

    mine = pl.ds(pl.multiple_of((2 * x + c) * T, T), T)

    def weigh(s):
        weighted = gblk[s, :, mine].astype(F32) * ratio_of(lt[s])
        wbt[:, s * T:(s + 1) * T] = weighted.T.astype(BF16)

    for s in range(3):
        weigh(s)
    r1.wait_recv()
    psum[xp, 0:8] += xr[0]
    r3 = send(psum.at[xp, 0:8], xr.at[4], right)
    l1.wait_recv()
    psum[xm, 8:16] += xr[1]
    l3 = send(psum.at[xm, 8:16], xr.at[5], left)
    b_y = step_b(1, b_y)
    for s in range(3):
        g_s[s].wait_recv()
        weigh(3 + s)

    def rows_of(lo, hi, i):
        return gblk[lo:hi, :, pl.ds(pl.multiple_of(i * T, T), T)].reshape((hi - lo) * T, T)

    def factor_first(i, _):
        yf[i] = jnp.dot(wbt[:, 0:6 * T], rows_of(0, 6, i), preferred_element_type=F32)
        return 0

    def factor_rest(i, _):
        yf[i] += jnp.dot(wbt[:, 6 * T:8 * T], rows_of(6, 8, i), preferred_element_type=F32)
        return 0

    lax.fori_loop(0, Y, factor_first, 0)
    arrived(y_counts)
    cz[0] = jnp.sum(cy[...], axis=0)
    z_counts = [send(cz.at[0], cz.at[1 + i], to) for i, to in enumerate(zhs)]
    arrived([f_r, f_l])
    g_s.append(send(gblk.at[6], gblk.at[7], sib))
    weigh(6)
    g_s[3].wait_recv()
    weigh(7)
    lax.fori_loop(0, Y, factor_rest, 0)
    f_y = step_f(0, None)
    b_y = step_b(2, b_y)

    l2.wait_recv()
    r3.wait_recv()
    ya[0:4] = (psum[x, 0:8] + xr[3] + xr[4]).reshape(4, 64, T)
    r2.wait_recv()
    l3.wait_recv()
    ya[4:8] = (psum[x, 8:16] + xr[2] + xr[5]).reshape(4, 64, T)
    a_y = step_a(0, None)
    arrived(w_z)
    zp, zm = lax.rem(zh + 1, ZH), lax.rem(zh + 3, ZH)
    w_z = [
        send(wbuf.at[0:4, zm, c, part], wbuf.at[0:4, zm, c, part], fore),
        send(wbuf.at[4:8, zp, c, part], wbuf.at[4:8, zp, c, part], back),
    ]
    f_y = step_f(1, f_y)
    b_y = step_b(3, b_y)
    a_y = step_a(1, a_y)
    arrived(z_counts)
    cl[0] = jnp.sum(cz[...], axis=0)
    l_counts = [send(cl.at[0], cl.at[1 + i], to) for i, to in enumerate(zls)]
    f_y = step_f(2, f_y)

    def quarter(q, lo=0, hi=Y):
        rows = pl.ds(pl.multiple_of(32 * q, 32), 32)
        return wbuf.at[lo:hi, :, c, rows]

    arrived(w_z)
    w_x = [send(quarter(x), quarter(x), right), send(quarter(x), quarter(x), left)]
    w_s = [send(quarter(x), quarter(x), sib)]

    arrived(b_y)
    xb[...] = jnp.swapaxes((yb[y] + ybr[3] + ybl[3]).reshape(2, X, 32, T), 0, 1)
    b_x = [send(xb.at[lax.rem(x + 1 + i, X)], xbr.at[1 + i], (to)) for i, to in enumerate([right, dev(dx=2), left])]
    xbr[0] = xb[x]
    a_y = step_a(2, a_y)
    f_y = step_f(3, f_y)
    a_y = step_a(3, a_y)

    arrived(l_counts)
    total = cl[0] + cl[1] + cl[2]
    valid = jnp.sum(total[0:8], axis=0, keepdims=True)
    seqs = jnp.sum(total[8:16], axis=0, keepdims=True)
    scale_row = valid / seqs
    scale = jnp.max(scale_row)

    arrived(w_x)
    w_x = [send(quarter(xm, 0, 4), quarter(xm, 0, 4), right), send(quarter(xp, 4, 8), quarter(xp, 4, 8), left)]
    w_s += [send(quarter(xm), quarter(xm), sib), send(quarter(xp), quarter(xp), sib)]

    arrived(f_y)
    zf[...] = (yf[y] + yfr[3] + yfl[3]).T.reshape(ZH, 32, T)
    f_z = [send(zf.at[lax.rem(zh + 1 + i, ZH)], zfr.at[1 + i], to) for i, to in enumerate(zhs)]
    zfr[0] = zf[zh]
    arrived(b_x)
    zw[0:2] = xbr[0] + xbr[1] + xbr[2] + xbr[3]
    arrived(a_y)
    zw[2:4] = (ya[y] + yar[3] + yal[3]).reshape(2, 32, T)
    w_zs = [send(zw.at[lax.rem(zh + 1 + i, ZH)], zwr.at[1 + i], to) for i, to in enumerate(zhs)]
    zwr[0] = zw[zh]

    arrived(w_x)
    w_s.append(send(quarter(xo), quarter(xo), sib))

    def product(i):
        out = lax.dot_general(
            sgs[...], wbuf[i].reshape(1024, T), (((1,), (1,)), ((), ())), preferred_element_type=F32
        )
        grad_in[:, i * 1024:(i + 1) * 1024] = (scale * out).astype(BF16)

    arrived(f_z)
    lr[0, 32:64] = zfr[0] + zfr[1] + zfr[2] + zfr[3]
    arrived(w_zs)
    lr[0, 0:32] = zwr[0] + zwr[1] + zwr[2] + zwr[3]
    l_sums = [send(lr.at[0], lr.at[1 + i], to) for i, to in enumerate(zls)]
    arrived(w_s)
    for i in range(3):
        product(i)
    arrived(l_sums)
    done = lr[0] + lr[1] + lr[2]
    finw[...] = done[0:32]
    finf[...] = done[32:64].reshape(2, 16, T)
    slot = 2 * x + c
    last = [send(finw, fw.at[x], to) for to in same]
    last += [send(finf.at[c], ff.at[slot], to) for to in same]
    last += [send(finf.at[1 - c], ff.at[slot], to) for to in other]
    fw[x] = done[0:32]
    ff[slot] = finf[c]
    for i in range(3, 8):
        product(i)
    arrived(last)
    wgrad[...] = scale * fw[...].reshape(T, T).T
    for g in range(8):
        factor[:, g * T:(g + 1) * T] = ff[g] / seqs
    for copy in sent:
        copy.wait_send()


def shards(activations, out_grad, key_weight, lengths):
    sems = 136
    hbm = pl.BlockSpec(memory_space=pltpu.HBM)
    vmem = pl.BlockSpec(memory_space=pltpu.VMEM)
    return pl.pallas_call(
        kernel,
        out_shape=(
            jax.ShapeDtypeStruct((T, 8192), BF16),
            jax.ShapeDtypeStruct((T, T), F32),
            jax.ShapeDtypeStruct((16, FBLK), F32),
        ),
        in_specs=[hbm, hbm, hbm, hbm],
        out_specs=(vmem, vmem, vmem),
        scratch_shapes=[
            pltpu.VMEM((32, 2, T, T), BF16),
            pltpu.VMEM((2, T, T), BF16),
            pltpu.VMEM((T, T), BF16),
            pltpu.VMEM((X, 16, 32, T), F32),
            pltpu.VMEM((6, 8, 32, T), F32),
            pltpu.VMEM((Y, 256, T), F32),
            pltpu.VMEM((4, 256, T), F32),
            pltpu.VMEM((4, 256, T), F32),
            pltpu.VMEM((Y, 64, T), F32),
            pltpu.VMEM((4, 64, T), F32),
            pltpu.VMEM((4, 64, T), F32),
            pltpu.VMEM((Y, T, T), F32),
            pltpu.VMEM((4, T, T), F32),
            pltpu.VMEM((4, T, T), F32),
            pltpu.VMEM((X, 2, 32, T), F32),
            pltpu.VMEM((X, 2, 32, T), F32),
            pltpu.VMEM((8, T, FBLK), BF16),
            pltpu.VMEM((T, 8 * T), BF16),
            pltpu.VMEM((8, 8, T), jnp.int32),
            pltpu.VMEM((Y, 16, T), F32),
            pltpu.VMEM((ZH, 16, T), F32),
            pltpu.VMEM((ZL, 16, T), F32),
            pltpu.VMEM((Y, ZH, 2, T, T), BF16),
            pltpu.VMEM((ZH, 32, T), F32),
            pltpu.VMEM((ZH, 32, T), F32),
            pltpu.VMEM((ZH, 32, T), F32),
            pltpu.VMEM((ZH, 32, T), F32),
            pltpu.VMEM((ZL, 64, T), F32),
            pltpu.VMEM((32, T), F32),
            pltpu.VMEM((2, 16, T), F32),
            pltpu.VMEM((X, 32, T), F32),
            pltpu.VMEM((8, 16, T), F32),
            pltpu.VMEM((T, T), BF16),
            pltpu.SMEM((1, 8), jnp.int32),
            pltpu.SemaphoreType.DMA((sems,)),
            pltpu.SemaphoreType.DMA((sems,)),
            pltpu.SemaphoreType.DMA((8,)),
        ],
        compiler_params=pltpu.CompilerParams(
            collective_id=0, has_side_effects=True, vmem_limit_bytes=48 * 1024 * 1024
        ),
    )(*[pltpu.with_memory_space_constraint(a, pltpu.HBM) for a in (activations, out_grad, key_weight, lengths)])


def solution(mesh):
    in_specs = (
        P(("rep", "fsdp"), None),
        P(("rep", "fsdp"), None),
        P("fsdp", None),
        P(("rep", "fsdp"), None),
    )
    out_specs = (P(("rep", "fsdp"), None), P("fsdp", None), P("fsdp", None))
    return jax.shard_map(shards, mesh=mesh, in_specs=in_specs, out_specs=out_specs, check_vma=False)
```

time: 92.4 us -> 74.6 us (0.81)
  Pallas kernels: 85.1 us -> 71.2 us
  local copies, waits for them, and re-layouts: 6.33 us -> 2.58 us
    pallas_call x1, Pallas kernels: 85.1 us -> 71.2 us  [shards(): pl.pallas_call(kernel, out_shape=(jax.ShapeDtypeStruct((T, 8192), BF16),...]
    unnamed x11 -> x3, local copies, waits for them, and re-layouts: 6.33 us -> 2.58 us
where the time goes in v2:
time: 74.6 us; the launch traced here: 74.4 us
  Pallas kernels  71.2 us (95%)
  local copies, waits for them, and re-layouts  2.58 us (3%)
    pallas_call x1, Pallas kernels, shards(): pl.pallas_call(kernel, out_shape=(jax.ShapeDtypeStruct((T, 8192), BF16),...  71.2 us
    unnamed x3, local copies, waits for them, and re-layouts  2.58 us

profile of v2, /device:TPU:1, one launch (start us, length us, event | category | flops | bytes accessed | tf_op | source)
XLA Modules:
  0.0 74.4 jit_solution(15960529735981283127)
XLA Ops:
  0.6 71.2 %shard_map.67 = (bf16[128,8192]{1,0:T(8,128)(2,1)S(1)}, f32[128,128]{1,0:T(8,128)S(1)}, f32[16,1024]{1,0:T(8,128)S(1)}) custom-call(bf16[128,8192]{1,0:T(8,128)(2,1)} %act.1, bf16[128,128]{1,0:T(8,128)(2,1)} %og.1, bf16[128,128]{1,0:T(8,128)(2,1)} %kw.1, s32[1,8]{1,0:T(1,128)} %lens.1), custom_call_target="tpu_custom_call" | custom-call | tf_op jit(solution)/shard_map/pallas_call | solution.py:360
  71.8 1.3 %copy.10 = bf16[128,8192]{1,0:T(8,128)(2,1)} copy(bf16[128,8192]{1,0:T(8,128)(2,1)S(1)} %get-tuple-element.6) | data formatting | bytes 4194304
  73.2 0.6 copy.11
  73.8 0.6 copy.12

commit v3 on v2

--- a/solution.py
+++ b/solution.py
@@ -75,7 +75,10 @@
         pl.semaphore_signal(barrier, inc=1, device_id=peer, device_id_type=MESH)
 
     def cols(i, half, core):
-        b = lax.div(i, 2) * 8 + half * 4 + lax.rem(i, 2) * 2 + core
+        if half == 0:
+            b = lax.rem(i, 8) * 8 + lax.div(i, 8) * 2 + core
+        else:
+            b = lax.div(i, 2) * 8 + 4 + lax.rem(i, 2) * 2 + core
         return act.at[:, pl.ds(pl.multiple_of(b * T, T), T)]
 
     for half in range(2):
@@ -91,6 +94,35 @@
     w_copy = pltpu.make_async_copy(kw.at[part], wbuf.at[y, zh, c, part], ls.at[2])
     w_copy.start()
 
+    pl.semaphore_wait(barrier, len(peers))
+
+    act_k = count[0]
+    count[0] += 2
+
+    def swap(half):
+        k = act_k + half
+
+        def start(i, _):
+            pltpu.make_async_remote_copy(
+                src_ref=cols(i, half, 1 - c), dst_ref=abuf.at[16 * half + i, 1], send_sem=ss.at[k], recv_sem=rs.at[k],
+                device_id=sib, device_id_type=MESH,
+            ).start()
+            return 0
+
+        lax.fori_loop(0, 16, start, 0)
+        part = abuf.at[16 * half:16 * half + 16]
+        whole = pltpu.make_async_remote_copy(
+            src_ref=part.at[:, 0], dst_ref=part.at[:, 1], send_sem=ss.at[k], recv_sem=rs.at[k],
+            device_id=sib, device_id_type=MESH,
+        )
+        sent.append(whole)
+        return whole
+
+    g_r = send(act.at[:, 0:FBLK], gblk.at[1], right)
+    g_l = send(act.at[:, 0:FBLK], gblk.at[2], left)
+    swap_b = swap(0)
+    swap_a = swap(1)
+    w_y = [send(kw.at[part], wbuf.at[y, zh, c, part], to) for to in ys]
     lens_copy.wait()
     row = lax.broadcasted_iota(jnp.int32, (8, T), 0)
     tile = jnp.zeros((8, T), jnp.int32)
@@ -101,37 +133,7 @@
     scaled = ogv[...].astype(F32) * ratio_of(tile)
     sgs[...] = scaled.astype(BF16)
     sgt[0] = scaled.T.astype(BF16)
-
-    pl.semaphore_wait(barrier, len(peers))
-
-    act_k = count[0]
-    count[0] += 2
-
-    def swap(half):
-        k = act_k + half
-
-        def start(i, _):
-            pltpu.make_async_remote_copy(
-                src_ref=cols(i, half, 1 - c), dst_ref=abuf.at[16 * half + i, 1], send_sem=ss.at[k], recv_sem=rs.at[k],
-                device_id=sib, device_id_type=MESH,
-            ).start()
-            return 0
-
-        lax.fori_loop(0, 16, start, 0)
-        part = abuf.at[16 * half:16 * half + 16]
-        whole = pltpu.make_async_remote_copy(
-            src_ref=part.at[:, 0], dst_ref=part.at[:, 1], send_sem=ss.at[k], recv_sem=rs.at[k],
-            device_id=sib, device_id_type=MESH,
-        )
-        sent.append(whole)
-        return whole
-
     s_copy = send(sgt.at[0], sgt.at[1], sib)
-    swap_a = swap(1)
-    g_r = send(act.at[:, 0:FBLK], gblk.at[1], right)
-    g_l = send(act.at[:, 0:FBLK], gblk.at[2], left)
-    swap_b = swap(0)
-    w_y = [send(kw.at[part], wbuf.at[y, zh, c, part], to) for to in ys]
     l_copies = [send(lt.at[0], lt.at[1 + i], to) for i, to in enumerate(group)]
 
     own_all.wait()
@@ -142,7 +144,7 @@
         return jnp.dot(heads, abuf[i].reshape(2 * T, T), preferred_element_type=F32)
 
     def block_b(i, _):
-        yb[lax.div(i, 2), pl.ds(pl.multiple_of(lax.rem(i, 2) * T, T), T)] = block(i)
+        yb[lax.div(i, 8), lax.rem(i, 8)] = block(i)
         return 0
 
     def block_a(i, _):
@@ -150,7 +152,7 @@
         return 0
 
     def y_step(buf, up_buf, down_buf, s, before):
-        n = buf.shape[1] // 2
+        n = buf.shape[-2] // 2
         t = 4 - s
         hi, lo = lax.rem(y + t, Y), lax.rem(y + Y - t, Y)
         if s == 0:
@@ -172,8 +174,8 @@
         b = send(buf.at[lo], down_buf.at[s], down)
         return [a, b]
 
-    def step_b(s, before):
-        return y_step(yb, ybr, ybl, s, before)
+    def step_b(k, s, before):
+        return y_step(yb.at[k], ybr.at[k], ybl.at[k], s, before)
 
     def step_a(s, before):
         return y_step(ya, yar, yal, s, before)
@@ -182,31 +184,34 @@
         return y_step(yf, yfr, yfl, s, before)
 
     xp, xm, xo = lax.rem(x + 1, X), lax.rem(x + 3, X), lax.rem(x + 2, X)
+    swap_b.wait_recv()
+    lax.fori_loop(0, 8, block_b, 0, unroll=4)
+    b0 = step_b(0, 0, None)
+    lax.fori_loop(8, 16, block_b, 0, unroll=4)
+    b1 = step_b(1, 0, None)
     swap_a.wait_recv()
-    lax.fori_loop(0, 16, block_a, 0)
+    lax.fori_loop(0, 16, block_a, 0, unroll=4)
     r1 = send(psum.at[xo, 0:8], xr.at[0], right)
     l1 = send(psum.at[xo, 8:16], xr.at[1], left)
     blk_copy.wait()
     g_s = [send(gblk.at[0], gblk.at[3], sib)]
-    swap_b.wait_recv()
-    lax.fori_loop(0, 16, block_b, 0)
-    b_y = step_b(0, None)
-
+    w_copy.wait()
+    arrived(w_y)
+    w_z = [
+        send(wbuf.at[:, zh, c, part], wbuf.at[:, zh, c, part], fore),
+        send(wbuf.at[:, zh, c, part], wbuf.at[:, zh, c, part], back),
+    ]
     g_r.wait_recv()
     f_r = send(gblk.at[1, 0:64], gblk.at[6, 0:64], right)
     g_l.wait_recv()
     f_l = send(gblk.at[2, 64:128], gblk.at[6, 64:128], left)
     g_s.append(send(gblk.at[1], gblk.at[4], sib))
     g_s.append(send(gblk.at[2], gblk.at[5], sib))
+
+    b0 = step_b(0, 1, b0)
+    b1 = step_b(1, 1, b1)
     r2 = send(psum.at[xp, 8:16], xr.at[2], right)
     l2 = send(psum.at[xm, 0:8], xr.at[3], left)
-
-    w_copy.wait()
-    arrived(w_y)
-    w_z = [
-        send(wbuf.at[:, zh, c, part], wbuf.at[:, zh, c, part], fore),
-        send(wbuf.at[:, zh, c, part], wbuf.at[:, zh, c, part], back),
-    ]
 
     arrived(l_copies)
     every = lt[...]
@@ -220,43 +225,49 @@
         weighted = gblk[s, :, mine].astype(F32) * ratio_of(lt[s])
         wbt[:, s * T:(s + 1) * T] = weighted.T.astype(BF16)
 
+    def rows_of(lo, hi, i):
+        return gblk[lo:hi, :, pl.ds(pl.multiple_of(i * T, T), T)].reshape((hi - lo) * T, T)
+
+    def factor_first(i, _):
+        yf[i] = jnp.dot(wbt[:, 0:6 * T], rows_of(0, 6, i), preferred_element_type=F32)
+        return 0
+
+    def factor_rest(i, _):
+        yf[i] += jnp.dot(wbt[:, 6 * T:8 * T], rows_of(6, 8, i), preferred_element_type=F32)
+        return 0
+
     for s in range(3):
         weigh(s)
+    for s in range(3):
+        g_s[s].wait_recv()
+        weigh(3 + s)
+    lax.fori_loop(0, Y, factor_first, 0, unroll=4)
+    arrived([f_r, f_l])
+    g_s.append(send(gblk.at[6], gblk.at[7], sib))
     r1.wait_recv()
     psum[xp, 0:8] += xr[0]
     r3 = send(psum.at[xp, 0:8], xr.at[4], right)
     l1.wait_recv()
     psum[xm, 8:16] += xr[1]
     l3 = send(psum.at[xm, 8:16], xr.at[5], left)
-    b_y = step_b(1, b_y)
-    for s in range(3):
-        g_s[s].wait_recv()
-        weigh(3 + s)
-
-    def rows_of(lo, hi, i):
-        return gblk[lo:hi, :, pl.ds(pl.multiple_of(i * T, T), T)].reshape((hi - lo) * T, T)
-
-    def factor_first(i, _):
-        yf[i] = jnp.dot(wbt[:, 0:6 * T], rows_of(0, 6, i), preferred_element_type=F32)
-        return 0
-
-    def factor_rest(i, _):
-        yf[i] += jnp.dot(wbt[:, 6 * T:8 * T], rows_of(6, 8, i), preferred_element_type=F32)
-        return 0
-
-    lax.fori_loop(0, Y, factor_first, 0)
+    b0 = step_b(0, 2, b0)
+    b1 = step_b(1, 2, b1)
+    weigh(6)
+    g_s[3].wait_recv()
+    weigh(7)
+    lax.fori_loop(0, Y, factor_rest, 0, unroll=4)
+    f_y = step_f(0, None)
+    b0 = step_b(0, 3, b0)
+    b1 = step_b(1, 3, b1)
     arrived(y_counts)
     cz[0] = jnp.sum(cy[...], axis=0)
     z_counts = [send(cz.at[0], cz.at[1 + i], to) for i, to in enumerate(zhs)]
-    arrived([f_r, f_l])
-    g_s.append(send(gblk.at[6], gblk.at[7], sib))
-    weigh(6)
-    g_s[3].wait_recv()
-    weigh(7)
-    lax.fori_loop(0, Y, factor_rest, 0)
-    f_y = step_f(0, None)
-    b_y = step_b(2, b_y)
-
+    arrived(w_z)
+    zp, zm = lax.rem(zh + 1, ZH), lax.rem(zh + 3, ZH)
+    w_z = [
+        send(wbuf.at[0:4, zm, c, part], wbuf.at[0:4, zm, c, part], fore),
+        send(wbuf.at[4:8, zp, c, part], wbuf.at[4:8, zp, c, part], back),
+    ]
     l2.wait_recv()
     r3.wait_recv()
     ya[0:4] = (psum[x, 0:8] + xr[3] + xr[4]).reshape(4, 64, T)
@@ -264,15 +275,14 @@
     l3.wait_recv()
     ya[4:8] = (psum[x, 8:16] + xr[2] + xr[5]).reshape(4, 64, T)
     a_y = step_a(0, None)
-    arrived(w_z)
-    zp, zm = lax.rem(zh + 1, ZH), lax.rem(zh + 3, ZH)
-    w_z = [
-        send(wbuf.at[0:4, zm, c, part], wbuf.at[0:4, zm, c, part], fore),
-        send(wbuf.at[4:8, zp, c, part], wbuf.at[4:8, zp, c, part], back),
-    ]
     f_y = step_f(1, f_y)
-    b_y = step_b(3, b_y)
     a_y = step_a(1, a_y)
+    b_x = []
+    for k, arriving in enumerate([b0, b1]):
+        arrived(arriving)
+        xb[k] = (yb[k, y] + ybr[k, 3] + ybl[k, 3]).reshape(X, 32, T)
+        b_x += [send(xb.at[k, lax.rem(x + 1 + i, X)], xbr.at[k, 1 + i], to) for i, to in enumerate([right, dev(dx=2), left])]
+        xbr[k, 0] = xb[k, x]
     arrived(z_counts)
     cl[0] = jnp.sum(cz[...], axis=0)
     l_counts = [send(cl.at[0], cl.at[1 + i], to) for i, to in enumerate(zls)]
@@ -285,11 +295,6 @@
     arrived(w_z)
     w_x = [send(quarter(x), quarter(x), right), send(quarter(x), quarter(x), left)]
     w_s = [send(quarter(x), quarter(x), sib)]
-
-    arrived(b_y)
-    xb[...] = jnp.swapaxes((yb[y] + ybr[3] + ybl[3]).reshape(2, X, 32, T), 0, 1)
-    b_x = [send(xb.at[lax.rem(x + 1 + i, X)], xbr.at[1 + i], (to)) for i, to in enumerate([right, dev(dx=2), left])]
-    xbr[0] = xb[x]
     a_y = step_a(2, a_y)
     f_y = step_f(3, f_y)
     a_y = step_a(3, a_y)
@@ -301,20 +306,19 @@
     scale_row = valid / seqs
     scale = jnp.max(scale_row)
 
-    arrived(w_x)
-    w_x = [send(quarter(xm, 0, 4), quarter(xm, 0, 4), right), send(quarter(xp, 4, 8), quarter(xp, 4, 8), left)]
-    w_s += [send(quarter(xm), quarter(xm), sib), send(quarter(xp), quarter(xp), sib)]
-
     arrived(f_y)
     zf[...] = (yf[y] + yfr[3] + yfl[3]).T.reshape(ZH, 32, T)
     f_z = [send(zf.at[lax.rem(zh + 1 + i, ZH)], zfr.at[1 + i], to) for i, to in enumerate(zhs)]
     zfr[0] = zf[zh]
     arrived(b_x)
-    zw[0:2] = xbr[0] + xbr[1] + xbr[2] + xbr[3]
+    zw[0:2] = xbr[:, 0] + xbr[:, 1] + xbr[:, 2] + xbr[:, 3]
     arrived(a_y)
     zw[2:4] = (ya[y] + yar[3] + yal[3]).reshape(2, 32, T)
     w_zs = [send(zw.at[lax.rem(zh + 1 + i, ZH)], zwr.at[1 + i], to) for i, to in enumerate(zhs)]
     zwr[0] = zw[zh]
+    arrived(w_x)
+    w_x = [send(quarter(xm, 0, 4), quarter(xm, 0, 4), right), send(quarter(xp, 4, 8), quarter(xp, 4, 8), left)]
+    w_s += [send(quarter(xm), quarter(xm), sib), send(quarter(xp), quarter(xp), sib)]
 
     arrived(w_x)
     w_s.append(send(quarter(xo), quarter(xo), sib))
@@ -354,7 +358,7 @@
 
 
 def shards(activations, out_grad, key_weight, lengths):
-    sems = 136
+    sems = 152
     hbm = pl.BlockSpec(memory_space=pltpu.HBM)
     vmem = pl.BlockSpec(memory_space=pltpu.VMEM)
     return pl.pallas_call(
@@ -372,17 +376,17 @@
             pltpu.VMEM((T, T), BF16),
             pltpu.VMEM((X, 16, 32, T), F32),
             pltpu.VMEM((6, 8, 32, T), F32),
-            pltpu.VMEM((Y, 256, T), F32),
-            pltpu.VMEM((4, 256, T), F32),
-            pltpu.VMEM((4, 256, T), F32),
+            pltpu.VMEM((2, Y, T, T), F32),
+            pltpu.VMEM((2, 4, T, T), F32),
+            pltpu.VMEM((2, 4, T, T), F32),
             pltpu.VMEM((Y, 64, T), F32),
             pltpu.VMEM((4, 64, T), F32),
             pltpu.VMEM((4, 64, T), F32),
             pltpu.VMEM((Y, T, T), F32),
             pltpu.VMEM((4, T, T), F32),
             pltpu.VMEM((4, T, T), F32),
-            pltpu.VMEM((X, 2, 32, T), F32),
-            pltpu.VMEM((X, 2, 32, T), F32),
+            pltpu.VMEM((2, X, 32, T), F32),
+            pltpu.VMEM((2, X, 32, T), F32),
             pltpu.VMEM((8, T, FBLK), BF16),
             pltpu.VMEM((T, 8 * T), BF16),
             pltpu.VMEM((8, 8, T), jnp.int32),

time: 74.6 us -> 73 us (0.979)
  Pallas kernels: 71.2 us -> 69.6 us
    pallas_call x1, Pallas kernels: 71.2 us -> 69.6 us  [shards(): pl.pallas_call(kernel, out_shape=(jax.ShapeDtypeStruct((T, 8192), BF16),...]
where the time goes in v3:
time: 73 us; the launch traced here: 72.9 us
  Pallas kernels  69.6 us (95%)
  local copies, waits for them, and re-layouts  2.58 us (4%)
    pallas_call x1, Pallas kernels, shards(): pl.pallas_call(kernel, out_shape=(jax.ShapeDtypeStruct((T, 8192), BF16),...  69.6 us
    unnamed x3, local copies, waits for them, and re-layouts  2.58 us

profile of v3, /device:TPU:1, one launch (start us, length us, event | category | flops | bytes accessed | tf_op | source)
XLA Modules:
  0.0 72.9 jit_solution(16186394357918315507)
XLA Ops:
  0.6 69.6 %shard_map.67 = (bf16[128,8192]{1,0:T(8,128)(2,1)S(1)}, f32[128,128]{1,0:T(8,128)S(1)}, f32[16,1024]{1,0:T(8,128)S(1)}) custom-call(bf16[128,8192]{1,0:T(8,128)(2,1)} %act.1, bf16[128,128]{1,0:T(8,128)(2,1)} %og.1, bf16[128,128]{1,0:T(8,128)(2,1)} %kw.1, s32[1,8]{1,0:T(1,128)} %lens.1), custom_call_target="tpu_custom_call" | custom-call | tf_op jit(solution)/shard_map/pallas_call | solution.py:364
  70.3 1.3 %copy.10 = bf16[128,8192]{1,0:T(8,128)(2,1)} copy(bf16[128,8192]{1,0:T(8,128)(2,1)S(1)} %get-tuple-element.6) | data formatting | bytes 4194304
  71.6 0.6 copy.11
  72.2 0.6 copy.12

commit v4 on v3

--- a/solution.py
+++ b/solution.py
@@ -331,22 +331,24 @@
 
     arrived(f_z)
     lr[0, 32:64] = zfr[0] + zfr[1] + zfr[2] + zfr[3]
+    l_f = [send(lr.at[0, 32:64], lr.at[1 + i, 32:64], to) for i, to in enumerate(zls)]
     arrived(w_zs)
     lr[0, 0:32] = zwr[0] + zwr[1] + zwr[2] + zwr[3]
-    l_sums = [send(lr.at[0], lr.at[1 + i], to) for i, to in enumerate(zls)]
+    l_w = [send(lr.at[0, 0:32], lr.at[1 + i, 0:32], to) for i, to in enumerate(zls)]
     arrived(w_s)
     for i in range(3):
         product(i)
-    arrived(l_sums)
-    done = lr[0] + lr[1] + lr[2]
-    finw[...] = done[0:32]
-    finf[...] = done[32:64].reshape(2, 16, T)
     slot = 2 * x + c
-    last = [send(finw, fw.at[x], to) for to in same]
+    arrived(l_f)
+    finf[...] = (lr[0, 32:64] + lr[1, 32:64] + lr[2, 32:64]).reshape(2, 16, T)
+    last = [send(finf.at[1 - c], ff.at[slot], to) for to in other]
     last += [send(finf.at[c], ff.at[slot], to) for to in same]
-    last += [send(finf.at[1 - c], ff.at[slot], to) for to in other]
-    fw[x] = done[0:32]
     ff[slot] = finf[c]
+    arrived(l_w)
+    done = lr[0, 0:32] + lr[1, 0:32] + lr[2, 0:32]
+    finw[...] = done
+    last += [send(finw, fw.at[x], to) for to in same]
+    fw[x] = done
     for i in range(3, 8):
         product(i)
     arrived(last)

time: 73 us -> 70.6 us (0.967)
  Pallas kernels: 69.6 us -> 67.2 us
    pallas_call x1, Pallas kernels: 69.6 us -> 67.2 us  [shards(): pl.pallas_call(kernel, out_shape=(jax.ShapeDtypeStruct((T, 8192), BF16),...]
where the time goes in v4:
time: 70.6 us; the launch traced here: 70.4 us
  Pallas kernels  67.2 us (95%)
  local copies, waits for them, and re-layouts  2.58 us (4%)
    pallas_call x1, Pallas kernels, shards(): pl.pallas_call(kernel, out_shape=(jax.ShapeDtypeStruct((T, 8192), BF16),...  67.2 us
    unnamed x3, local copies, waits for them, and re-layouts  2.58 us

profile of v4, /device:TPU:1, one launch (start us, length us, event | category | flops | bytes accessed | tf_op | source)
XLA Modules:
  0.0 70.4 jit_solution(8437981444531002611)
XLA Ops:
  0.6 67.2 %shard_map.67 = (bf16[128,8192]{1,0:T(8,128)(2,1)S(1)}, f32[128,128]{1,0:T(8,128)S(1)}, f32[16,1024]{1,0:T(8,128)S(1)}) custom-call(bf16[128,8192]{1,0:T(8,128)(2,1)} %act.1, bf16[128,128]{1,0:T(8,128)(2,1)} %og.1, bf16[128,128]{1,0:T(8,128)(2,1)} %kw.1, s32[1,8]{1,0:T(1,128)} %lens.1), custom_call_target="tpu_custom_call" | custom-call | tf_op jit(solution)/shard_map/pallas_call | solution.py:366
  67.8 1.3 %copy.10 = bf16[128,8192]{1,0:T(8,128)(2,1)} copy(bf16[128,8192]{1,0:T(8,128)(2,1)S(1)} %get-tuple-element.6) | data formatting | bytes 4194304
  69.2 0.6 copy.11
  69.8 0.6 copy.12

commit v5 on v4

--- a/solution.py
+++ b/solution.py
@@ -351,10 +351,11 @@
     fw[x] = done
     for i in range(3, 8):
         product(i)
-    arrived(last)
-    wgrad[...] = scale * fw[...].reshape(T, T).T
+    arrived(last[:7])
     for g in range(8):
         factor[:, g * T:(g + 1) * T] = ff[g] / seqs
+    arrived(last[7:])
+    wgrad[...] = scale * fw[...].reshape(T, T).T
     for copy in sent:
         copy.wait_send()
 

time: 70.6 us -> 70.6 us (level)
  no operation moved by 1% of the time
where the time goes in v5:
time: 70.6 us; the launch traced here: 70.4 us
  Pallas kernels  67.2 us (95%)
  local copies, waits for them, and re-layouts  2.58 us (4%)
    pallas_call x1, Pallas kernels, shards(): pl.pallas_call(kernel, out_shape=(jax.ShapeDtypeStruct((T, 8192), BF16),...  67.2 us
    unnamed x3, local copies, waits for them, and re-layouts  2.58 us

profile of v5, /device:TPU:1, one launch (start us, length us, event | category | flops | bytes accessed | tf_op | source)
XLA Modules:
  0.0 70.4 jit_solution(2214655313317048471)
XLA Ops:
  0.6 67.2 %shard_map.67 = (bf16[128,8192]{1,0:T(8,128)(2,1)S(1)}, f32[128,128]{1,0:T(8,128)S(1)}, f32[16,1024]{1,0:T(8,128)S(1)}) custom-call(bf16[128,8192]{1,0:T(8,128)(2,1)} %act.1, bf16[128,128]{1,0:T(8,128)(2,1)} %og.1, bf16[128,128]{1,0:T(8,128)(2,1)} %kw.1, s32[1,8]{1,0:T(1,128)} %lens.1), custom_call_target="tpu_custom_call" | custom-call | tf_op jit(solution)/shard_map/pallas_call | solution.py:367
  67.8 1.3 %copy.10 = bf16[128,8192]{1,0:T(8,128)(2,1)} copy(bf16[128,8192]{1,0:T(8,128)(2,1)S(1)} %get-tuple-element.6) | data formatting | bytes 4194304
  69.2 0.6 copy.11
  69.8 0.6 copy.12
